TPU v7x, 128 devices: a whole 4x4x4 slice. The times are simulated.
128 devices in a mesh: car: 8 (over z_hi, x), dom: 16 (over y, z_lo, core).
Axes of the slice: x: 4, y: 4, z: 4 (z_hi: 2, z_lo: 2; z = z_hi * 2 + z_lo), core: 2. Of those that a mesh axis runs over, the one named last changes fastest.
Arguments:
- points: bfloat16 [131072, 768], P(('car', 'dom')), parts along dimension 0, may hold values from -6 to 6
- norm_gain: float32 [768], replicated, may hold values from 0.25 to 1.75
- w_qkv: bfloat16 [768, 2304], replicated, may hold values from -0.12629537 to 0.12629537
- w_out: bfloat16 [768, 768], replicated, may hold values from -0.75 to 0.75
- w_cross_q: bfloat16 [768, 768], replicated, may hold values from -0.12629537 to 0.12629537
- w_cross_kv: bfloat16 [768, 1536], replicated, may hold values from -0.12629537 to 0.12629537
- w_cross_out: bfloat16 [768, 768], replicated, may hold values from -0.75 to 0.75
- live_blocks: int32 [128], P(('car', 'dom')), parts along dimension 0, may hold values from 4 to 8, as said below
- send_blocks: int32 [512], P(('car', 'dom')), parts along dimension 0, may hold values from 0 to 7, as said below
- neighbours: int32 [1024, 8], P(('car', 'dom')), parts along dimension 0, may hold values from 0 to 11, as said below
- neighbour_count: int32 [1024], P(('car', 'dom')), parts along dimension 0, may hold values from 2 to 8
- anchor_index: int32 [32768], P(('car', 'dom')), parts along dimension 0, may hold values from 0 to 1023, as said below
Outputs:
- mixed: bfloat16 [131072, 768], P(('car', 'dom')), parts along dimension 0
There are 8 independent parts, one for each index of `car`. A program takes and returns all parts, laid end to end along the dimension named above; an argument that names none is the same for every part. Nothing has to cross between parts.
Inputs may be any that keep to these rules, and one draw needn't show every extreme that they name: `live_blocks`: some partition of every car has all 8 blocks live. `send_blocks`: the 2 blocks of each list are distinct live blocks of the sending partition. `neighbours`: slot 0 of every block is the block itself; the first partition of a car names no block of a previous one and the last none of a next one; counted slots of a live block name live blocks. `anchor_index`: anchors lie in live blocks of their partition.
All inputs are finite; a program needn't handle non-finite values.
Results may differ from a plain program's by a relative error of at most 0.0086.
Values may be sent and summed in bfloat16 or wider, within the bound.
No kernel may reach another device: no remote copies, remote signals or barrier semaphores. Data moves between devices by JAX's collectives and lax.ppermute only.
A program may use at most 256 MiB of HBM per device.

v0:
```python
import jax
import jax.numpy as jnp
from jax import lax
from jax.sharding import PartitionSpec as P

HEADS = 12
BLK = 128
HB = 2


def extended_2(block, sides, width):
    for axis, dim in sides:
        count = lax.axis_size(axis)
        forward = [(i, i + 1) for i in range(count - 1)]
        backward = [(target, source) for source, target in forward]
        low = lax.ppermute(
            lax.slice_in_dim(block, block.shape[dim] - width, None, axis=dim), axis, forward
        )
        high = lax.ppermute(lax.slice_in_dim(block, 0, width, axis=dim), axis, backward)
        block = jnp.concatenate([low, block, high], axis=dim)
    return block


def normalize(points, norm_gain):
    floats = points.astype(jnp.float32)
    factor = lax.rsqrt(jnp.mean(floats * floats, axis=-1, keepdims=True) + 1e-06)
    return (floats * factor * norm_gain).astype(jnp.bfloat16)


def attend_batch(queries, key_rows, value_rows, key_valid):
    batch, row_count, model_width = queries.shape
    key_count = key_rows.shape[1]
    head_dim = model_width // HEADS
    query_heads = queries.reshape(batch, row_count, HEADS, head_dim)
    key_heads = key_rows.reshape(batch, key_count, HEADS, head_dim)
    value_heads = value_rows.reshape(batch, key_count, HEADS, head_dim)
    scores = jnp.einsum(
        "brhd,bkhd->bhrk", query_heads, key_heads, preferred_element_type=jnp.float32
    ) * head_dim ** (-0.5)
    scores = jnp.where(key_valid[:, None, None, :], scores, -1e30)
    row_max = jnp.max(scores, axis=-1, keepdims=True)
    expo = jnp.exp(scores - row_max)
    weights = (expo / jnp.sum(expo, axis=-1, keepdims=True)).astype(jnp.bfloat16)
    result = jnp.einsum("bhrk,bkhd->brhd", weights, value_heads, preferred_element_type=jnp.float32)
    return result.reshape(batch, row_count, model_width).astype(jnp.bfloat16)


def local(
    points,
    norm_gain,
    w_qkv,
    w_out,
    w_cross_q,
    w_cross_kv,
    w_cross_out,
    live_blocks,
    send_blocks,
    neighbours,
    neighbour_count,
    anchor_index,
):
    row_count, model_width = points.shape
    block_count = row_count // BLK
    group_size = 4
    normed = normalize(points, norm_gain)
    qkv = jnp.dot(normed, w_qkv, preferred_element_type=jnp.float32).astype(jnp.bfloat16)
    queries = qkv[:, :model_width]
    pair_blocks = qkv[:, model_width:].reshape(block_count, BLK, 2 * model_width)
    outgoing = pair_blocks[send_blocks]
    extended = extended_2(outgoing, (("dom", 0),), HB)
    remote = jnp.concatenate([extended[:HB], extended[3 * HB :]], axis=0)
    pair_table = jnp.concatenate([pair_blocks, remote], axis=0)
    slot_valid = jnp.arange(neighbours.shape[1])[None, :] < neighbour_count[:, None]

    def one_group(inputs):
        group_query, block_ids, group_valid = inputs
        tiles = pair_table[block_ids].reshape(group_size, -1, 2 * model_width)
        key_valid = jnp.repeat(group_valid, BLK, axis=1)
        return attend_batch(
            group_query, tiles[:, :, :model_width], tiles[:, :, model_width:], key_valid
        )

    group_count = block_count // group_size
    block_attn = lax.map(
        one_group,
        (
            queries.reshape(group_count, group_size, BLK, model_width),
            neighbours.reshape(group_count, group_size, -1),
            slot_valid.reshape(group_count, group_size, -1),
        ),
    )
    block_term = jnp.dot(
        block_attn.reshape(-1, model_width), w_out, preferred_element_type=jnp.float32
    )
    anchor_rows = normed[anchor_index]
    local_kv = jnp.dot(anchor_rows, w_cross_kv, preferred_element_type=jnp.float32).astype(
        jnp.bfloat16
    )
    anchor_kv = lax.all_gather(local_kv, "dom", axis=0, tiled=True)
    cross_query = jnp.dot(normed, w_cross_q, preferred_element_type=jnp.float32).astype(
        jnp.bfloat16
    )
    anchor_mask = jnp.ones((1, anchor_kv.shape[0]), bool)
    anchor_keys = anchor_kv[None, :, :model_width]
    anchor_values = anchor_kv[None, :, model_width:]

    def cross_group(group_query):
        return attend_batch(group_query[None], anchor_keys, anchor_values, anchor_mask)[0]

    cross_attn = lax.map(cross_group, cross_query.reshape(-1, group_size * BLK, model_width))
    cross_term = jnp.dot(
        cross_attn.reshape(-1, model_width), w_cross_out, preferred_element_type=jnp.float32
    )
    is_live = jnp.arange(row_count) // BLK < live_blocks[0]
    return jnp.where(is_live[:, None], block_term + cross_term, 0.0).astype(jnp.bfloat16)


def solution(mesh):
    in_specs = (
        P(("car", "dom"), None),
        P(),
        P(),
        P(),
        P(),
        P(),
        P(),
        P(("car", "dom")),
        P(("car", "dom")),
        P(("car", "dom"), None),
        P(("car", "dom")),
        P(("car", "dom")),
    )
    out_specs = P(("car", "dom"), None)
    return jax.shard_map(local, mesh=mesh, in_specs=in_specs, out_specs=out_specs, check_vma=False)
```

profile of v0, /device:TPU:1, one launch (start us, length us, event | category | flops | bytes accessed | tf_op | source)
XLA Modules:
  0.0 407.9 jit_solution(17363695349722959988)
XLA Ops:
  19.5 5.9 %convolution_convert_fusion = bf16[1024,2304]{1,0:T(8,128)(2,1)S(1)} fusion(bf16[1024,768]{1,0:T(8,128)(2,1)} %fusion.23, bf16[768,2304]{1,0:T(8,128)(2,1)S(1)} %copy-done), kind=kOutput, calls=%fused_computation.35 | convolution fusion | flops 3626237952 | bytes 9830400 | tf_op jit(solution)/shard_map/dot_general | solution.py:66
  47.2 24.1 %collective-permute-done = bf16[2,128,1536]{2,1,0:T(8,128)(2,1)} collective-permute-done((bf16[2,128,1536]{2,1,0:T(8,128)(2,1)}, bf16[2,128,1536]{2,1,0:T(8,128)(2,1)}, u32[]{:S(2)}, u32[]{:S(2)}) %collective-permute-start) | collective-permute-done | bytes 786464 | tf_op jit(solution)/shard_map/ppermute | solution.py:16
  76.6 133.5 %while.20 = (s32[]{:T(128)}, bf16[2,4,128,768]{3,2,1,0:T(8,128)(2,1)}, s32[2,4,8]{2,1,0:T(4,128)S(1)}, bf16[12,128,1536]{2,1,0:T(8,128)(2,1)}, pred[2,4,8]{2,1,0...) while((s32[]{:T(128)}, bf16[2,4,128,768]{3,2,1,0:T(8,128)(2,1)}, s32[2,4,8]{2,1,0:T(4,128)S(1)}, ...), condition=%wide.region_4.5_spmd, body=%wide.region_1.4_spmd.sunk | while | flops 1648756864 | bytes 165221392 | solution.py:84
  76.7 9.4 %gather_fusion = bf16[32,128,1536]{2,1,0:T(8,128)(2,1)} fusion(bf16[12,128,1536]{2,1,0:T(8,128)(2,1)} %get-tuple-element.217, s32[1024]{0:T(1024)S(1)} %pad_clamp_fusion.4), kind=kCustom, calls=%fused_computation.clone.1 | custom fusion | bytes 25165952 | tf_op jit(solution)/shard_map/while/body/eval_jaxpr/gather | solution.py:77
  86.1 10.4 %fusion.68 = (bf16[4,1024,768]{2,1,0:T(8,128)(2,1)}, bf16[4,1024,768]{2,1,0:T(8,128)(2,1)}) fusion(bf16[4,1024,1536]{2,1,0:T(8,128)(2,1)} %bitcast.94), kind=kLoop, calls=%fused_computation.60.clone.1 | loop fusion | bytes 25165824 | tf_op jit(solution)/shard_map/while/body/eval_jaxpr/slice | solution.py:80
  96.5 8.8 %copy.48 = bf16[4,1024,768]{1,2,0:T(8,128)(2,1)} copy(bf16[4,1024,768]{2,1,0:T(8,128)(2,1)} %get-tuple-element.190) | data formatting | bytes 12582912 | tf_op jit(solution)/shard_map/while
  105.8 15.1 %fusion.69 = (f32[4,12,128]{2,1,0:T(8,128)S(1)}, f32[4,12,128,1024]{3,2,1,0:T(8,128)}) fusion(pred[4,1024]{1,0:T(4,128)(4,1)S(1)} %bitcast.107, bf16[4,128,12,64]{1,3,2,0:T(8,128)(2,1)S(1)} %bitcast.97, bf16[4,1024,12,64]{1,3,2,0:T(8,128)(2,1)} %bitcast.95), kind=kOutput, calls=%fused_computation.61.clone.1 | convolution fusion | flops 830473216 | bytes 32272384 | tf_op jit(solution)/shard_map/while/body/eval_jaxpr/sub | solution.py:42
  120.9 8.7 %copy.45 = bf16[4,1024,768]{1,2,0:T(8,128)(2,1)} copy(bf16[4,1024,768]{2,1,0:T(8,128)(2,1)} %get-tuple-element.189) | data formatting | bytes 12582912 | tf_op jit(solution)/shard_map/while
  129.6 12.5 %fusion.70 = bf16[4,12,64,128]{3,2,1,0:T(8,128)(2,1)S(1)} fusion(bf16[4,1024,12,64]{1,3,2,0:T(8,128)(2,1)} %bitcast.96, f32[4,12,128,1024]{3,2,1,0:T(8,128)} %get-tuple-element.191, f32[4,12,128]{2,1,0:T(8,128)S(1)} %get-tuple-element.192), kind=kOutput, calls=%fused_computation.25.clone.1 | convolution fusion | flops 818282496 | bytes 32268288 | tf_op jit(solution)/shard_map/while/body/eval_jaxpr/bhrk,bkhd->brhd/dot_general | solution.py:44
  143.7 9.0 %gather_fusion = bf16[32,128,1536]{2,1,0:T(8,128)(2,1)} fusion(bf16[12,128,1536]{2,1,0:T(8,128)(2,1)} %get-tuple-element.217, s32[1024]{0:T(1024)S(1)} %pad_clamp_fusion.4), kind=kCustom, calls=%fused_computation.clone.1 | custom fusion | bytes 25165952 | tf_op jit(solution)/shard_map/while/body/eval_jaxpr/gather | solution.py:77
  152.7 10.3 %fusion.68 = (bf16[4,1024,768]{2,1,0:T(8,128)(2,1)}, bf16[4,1024,768]{2,1,0:T(8,128)(2,1)}) fusion(bf16[4,1024,1536]{2,1,0:T(8,128)(2,1)} %bitcast.94), kind=kLoop, calls=%fused_computation.60.clone.1 | loop fusion | bytes 25165824 | tf_op jit(solution)/shard_map/while/body/eval_jaxpr/slice | solution.py:80
  163.0 8.8 %copy.48 = bf16[4,1024,768]{1,2,0:T(8,128)(2,1)} copy(bf16[4,1024,768]{2,1,0:T(8,128)(2,1)} %get-tuple-element.190) | data formatting | bytes 12582912 | tf_op jit(solution)/shard_map/while
  172.3 15.1 %fusion.69 = (f32[4,12,128]{2,1,0:T(8,128)S(1)}, f32[4,12,128,1024]{3,2,1,0:T(8,128)}) fusion(pred[4,1024]{1,0:T(4,128)(4,1)S(1)} %bitcast.107, bf16[4,128,12,64]{1,3,2,0:T(8,128)(2,1)S(1)} %bitcast.97, bf16[4,1024,12,64]{1,3,2,0:T(8,128)(2,1)} %bitcast.95), kind=kOutput, calls=%fused_computation.61.clone.1 | convolution fusion | flops 830473216 | bytes 32272384 | tf_op jit(solution)/shard_map/while/body/eval_jaxpr/sub | solution.py:42
  187.4 8.7 %copy.45 = bf16[4,1024,768]{1,2,0:T(8,128)(2,1)} copy(bf16[4,1024,768]{2,1,0:T(8,128)(2,1)} %get-tuple-element.189) | data formatting | bytes 12582912 | tf_op jit(solution)/shard_map/while
  196.1 12.5 %fusion.70 = bf16[4,12,64,128]{3,2,1,0:T(8,128)(2,1)S(1)} fusion(bf16[4,1024,12,64]{1,3,2,0:T(8,128)(2,1)} %bitcast.96, f32[4,12,128,1024]{3,2,1,0:T(8,128)} %get-tuple-element.191, f32[4,12,128]{2,1,0:T(8,128)S(1)} %get-tuple-element.192), kind=kOutput, calls=%fused_computation.25.clone.1 | convolution fusion | flops 818282496 | bytes 32268288 | tf_op jit(solution)/shard_map/while/body/eval_jaxpr/bhrk,bkhd->brhd/dot_general | solution.py:44
  214.9 10.4 %fusion.31 = (bf16[4096,768]{1,0:T(8,128)(2,1)}, bf16[4096,768]{1,0:T(8,128)(2,1)}) fusion(bf16[4096,1536]{1,0:T(8,128)(2,1)} %all-gather.2.cloned.1.call-done), kind=kLoop, calls=%fused_computation.62 | loop fusion | bytes 25165824 | tf_op jit(solution)/shard_map/slice | solution.py:105
  225.3 8.7 %copy.24 = bf16[4096,768]{0,1:T(8,128)(2,1)} copy(bf16[4096,768]{1,0:T(8,128)(2,1)} %get-tuple-element.117) | data formatting | bytes 12582912 | tf_op jit(solution)/shard_map/while | solution.py:110
  234.0 8.9 %copy.25 = bf16[4096,768]{0,1:T(8,128)(2,1)} copy(bf16[4096,768]{1,0:T(8,128)(2,1)} %get-tuple-element.116) | data formatting | bytes 12582912 | tf_op jit(solution)/shard_map/while | solution.py:110
  242.9 152.7 %while.21 = (s32[]{:T(128)}, bf16[2,512,768]{2,1,0:T(8,128)(2,1)}, bf16[2,512,768]{2,1,0:T(8,128)(2,1)S(1)}, bf16[4096,768]{0,1:T(8,128)(2,1)}, bf16[4096,768]{0,1:T(8,128)(2,1)}, /*index=5*/s32[]{:T(128)}) while((s32[]{:T(128)}, bf16[2,512,768]{2,1,0:T(8,128)(2,1)}, bf16[2,512,768]{2,1,0:T(8,128)(2,1)S(1)}, bf16[4096,768]{0,1:T(8,128)(2,1)}, ...), condition=%wide.region_8.9_spmd, body=%wide.region_5.8_spmd.sunk | while | flops 6568677376 | bytes 221823568 | solution.py:110
  243.3 40.0 %fusion.74 = (f32[12,512]{1,0:T(8,128)S(1)}, f32[12,512,4096]{2,1,0:T(8,128)}) fusion(bf16[512,12,64]{0,2,1:T(8,128)(2,1)S(1)} %bitcast.99, bf16[4096,12,64]{0,2,1:T(8,128)(2,1)} %bitcast.105), kind=kOutput, calls=%fused_computation.59.clone.1 | convolution fusion | flops 3296727040 | bytes 107765760 | tf_op jit(solution)/shard_map/while/body/eval_jaxpr/sub | solution.py:42
  283.3 34.8 %fusion.75 = bf16[12,512,64]{1,2,0:T(8,128)(2,1)S(1)} fusion(bf16[4096,12,64]{0,2,1:T(8,128)(2,1)} %bitcast.106, f32[12,512,4096]{2,1,0:T(8,128)} %get-tuple-element.198, f32[12,512]{1,0:T(8,128)S(1)} %get-tuple-element.199), kind=kOutput, calls=%fused_computation.11.clone.1 | convolution fusion | flops 3271950336 | bytes 107765760 | tf_op jit(solution)/shard_map/while/body/eval_jaxpr/bhrk,bkhd->brhd/dot_general | solution.py:44
  319.6 40.0 %fusion.74 = (f32[12,512]{1,0:T(8,128)S(1)}, f32[12,512,4096]{2,1,0:T(8,128)}) fusion(bf16[512,12,64]{0,2,1:T(8,128)(2,1)S(1)} %bitcast.99, bf16[4096,12,64]{0,2,1:T(8,128)(2,1)} %bitcast.105), kind=kOutput, calls=%fused_computation.59.clone.1 | convolution fusion | flops 3296727040 | bytes 107765760 | tf_op jit(solution)/shard_map/while/body/eval_jaxpr/sub | solution.py:42
  359.6 34.8 %fusion.75 = bf16[12,512,64]{1,2,0:T(8,128)(2,1)S(1)} fusion(bf16[4096,12,64]{0,2,1:T(8,128)(2,1)} %bitcast.106, f32[12,512,4096]{2,1,0:T(8,128)} %get-tuple-element.198, f32[12,512]{1,0:T(8,128)S(1)} %get-tuple-element.199), kind=kOutput, calls=%fused_computation.11.clone.1 | convolution fusion | flops 3271950336 | bytes 107765760 | tf_op jit(solution)/shard_map/while/body/eval_jaxpr/bhrk,bkhd->brhd/dot_general | solution.py:44
  395.6 5.4 %select_convert_fusion = bf16[1024,768]{1,0:T(8,128)(2,1)} fusion(f32[1024,768]{1,0:T(8,128)} %fusion.33, bf16[1024,768]{1,0:T(8,128)(2,1)} %bitcast.109, bf16[768,768]{1,0:T(8,128)(2,1)} %param.22, pred[1024]{0:T(1024)(128)(4,1)S(1)} %copy-done.10), kind=kOutput, calls=%fused_computation.42 | convolution fusion | flops 1210318848 | bytes 7472128 | tf_op jit(solution)/shard_map/dot_general | solution.py:111
  (83 shorter events, 51.4 us)
Async XLA Ops:
  6.5 12.9 %copy-start = (bf16[768,2304]{1,0:T(8,128)(2,1)S(1)}, bf16[768,2304]{1,0:T(8,128)(2,1)}, u32[]{:S(2)}) copy-start(bf16[768,2304]{1,0:T(8,128)(2,1)} %param.18) | copy-start | bytes 10616836
  6.5 208.3 %all-gather.2.cloned.1.call-start = ((), (), s32[]{:S(2)}) async-start(), calls=%async_computation | async-start | bytes 13369344 | tf_op jit(solution)/shard_map/all_gather | solution.py:99
  25.3 2.1 copy-start.4
  25.3 0.7 copy-start.8
  29.3 12.2 %copy-start.9 = (s32[8]{0:T(128)S(1)}, s32[8]{0:T(128)}, u32[]{:S(2)}) copy-start(s32[8]{0:T(128)} %param.26) | copy-start | bytes 100
  32.0 39.4 %collective-permute-start = (bf16[2,128,1536]{2,1,0:T(8,128)(2,1)}, bf16[2,128,1536]{2,1,0:T(8,128)(2,1)}, u32[]{:S(2)}, u32[]{:S(2)}) collective-permute-start(bf16[2,128,1536]{2,1,0:T(8,128)(2,1)} %get-tuple-element.118), channel_id=1, source_target_pairs={{0,1},{1,2},{2,3},{3,4},{4,5},{5,6},{6,7},{7,8},{8,9},{9,10},{10,1... | collective-permute-start | bytes 2359304 | tf_op jit(solution)/shard_map/ppermute | solution.py:16
  36.9 34.5 %collective-permute-start.1 = (bf16[2,128,1536]{2,1,0:T(8,128)(2,1)}, bf16[2,128,1536]{2,1,0:T(8,128)(2,1)}, u32[]{:S(2)}, u32[]{:S(2)}) collective-permute-start(bf16[2,128,1536]{2,1,0:T(8,128)(2,1)} %get-tuple-element.119), channel_id=1, source_target_pairs={{1,0},{2,1},{3,2},{4,3},{5,4},{6,5},{7,6},{8,7},{9,8},{10,9},{11,1... | collective-permute-start | bytes 2359304 | tf_op jit(solution)/shard_map/ppermute | solution.py:19
  47.2 29.4 %copy-start.5 = (s32[8,8]{1,0:T(8,128)S(1)}, s32[8,8]{1,0:T(8,128)}, u32[]{:S(2)}) copy-start(s32[8,8]{1,0:T(8,128)} %param.25) | copy-start | bytes 772
  96.5 8.8 %copy-start.2 = (bf16[2,4,128,768]{3,2,1,0:T(8,128)(2,1)S(1)}, bf16[2,4,128,768]{3,2,1,0:T(8,128)(2,1)}, u32[]{:S(2)}) copy-start(bf16[2,4,128,768]{3,2,1,0:T(8,128)(2,1)} %get-tuple-element.219) | copy-start | bytes 4718596 | tf_op jit(solution)/shard_map/while
  129.6 12.8 %copy-start.6 = (bf16[2,4,128,768]{3,2,1,0:T(8,128)(2,1)S(1)}, bf16[2,4,128,768]{3,2,1,0:T(8,128)(2,1)}, u32[]{:S(2)}) copy-start(bf16[2,4,128,768]{3,2,1,0:T(8,128)(2,1)} %get-tuple-element.208) | copy-start | bytes 4718596 | tf_op jit(solution)/shard_map/while
  142.5 1.1 copy-start.7
  163.0 8.8 %copy-start.2 = (bf16[2,4,128,768]{3,2,1,0:T(8,128)(2,1)S(1)}, bf16[2,4,128,768]{3,2,1,0:T(8,128)(2,1)}, u32[]{:S(2)}) copy-start(bf16[2,4,128,768]{3,2,1,0:T(8,128)(2,1)} %get-tuple-element.219) | copy-start | bytes 4718596 | tf_op jit(solution)/shard_map/while
  196.1 12.8 %copy-start.6 = (bf16[2,4,128,768]{3,2,1,0:T(8,128)(2,1)S(1)}, bf16[2,4,128,768]{3,2,1,0:T(8,128)(2,1)}, u32[]{:S(2)}) copy-start(bf16[2,4,128,768]{3,2,1,0:T(8,128)(2,1)} %get-tuple-element.208) | copy-start | bytes 4718596 | tf_op jit(solution)/shard_map/while
  209.0 1.1 copy-start.7
  234.0 8.9 %copy-start.3 = (bf16[1024,768]{1,0:T(8,128)(2,1)S(1)}, bf16[1024,768]{1,0:T(8,128)(2,1)}, u32[]{:S(2)}) copy-start(bf16[1024,768]{1,0:T(8,128)(2,1)} %convolution_convert_fusion.2) | copy-start | bytes 4718596
  242.9 152.7 %copy-start.10 = (pred[1024]{0:T(1024)(128)(4,1)S(1)}, pred[1024]{0:T(1024)(128)(4,1)}, u32[]{:S(2)}) copy-start(pred[1024]{0:T(1024)(128)(4,1)} %fusion.24) | copy-start | bytes 3076
  395.6 5.4 %copy-start.1 = (bf16[768,2304]{1,0:T(8,128)(2,1)S(1)}, bf16[768,2304]{1,0:T(8,128)(2,1)}, u32[]{:S(2)}) copy-start(bf16[768,2304]{1,0:T(8,128)(2,1)} %param.18) | copy-start | bytes 10616836
Sparse Core Ops, SparseCore 0:
  19.6 87.9 all-gather.1
where the time goes:
time: 413 us; the launch traced here: 408 us
  matrix products  229 us (55%)
  local copies, waits for them, and re-layouts  122 us (30%)
  waiting for transfers between devices  24.2 us (6%)
  between operations  14.1 us (3%)
  other arithmetic  11.4 us (3%)
  starting transfers between devices  6.85 us (2%)
    sub x4, matrix products, attend_batch(): expo = jnp.exp(scores - row_max)  110 us
    dot_general x4, matrix products, attend_batch(): jnp.einsum('bhrk,bkhd->brhd', weights, value_heads, preferred_element_typ...  94.5 us
    while x20, local copies, waits for them, and re-layouts  37.4 us
    ppermute x1, waiting for transfers between devices, extended_2(): lax.ppermute(lax.slice_in_dim(block, block.shape[dim] - width, None, axis...  24.1 us
    slice x2, local copies, waits for them, and re-layouts, one_group(): tiles[:, :, :model_width]  20.7 us
    gather x2, local copies, waits for them, and re-layouts, one_group(): tiles = pair_table[block_ids].reshape(group_size, -1, 2 * model_width)  18.4 us
    while x2, local copies, waits for them, and re-layouts, local(): lax.map(cross_group, cross_query.reshape(-1, group_size * BLK, model_width))  17.6 us
    slice x1, local copies, waits for them, and re-layouts, local(): anchor_values = anchor_kv[None, :, model_width:]  10.4 us
  transfers between devices with their start and end apart: 3, of which 1 were waited for; matrix products, arithmetic and copies ran while one was open for 39% of the time, Pallas kernels for 0%

commit v1 on v0

v1 whole, which is shorter than its diff:
```python
import functools

import jax
import jax.numpy as jnp
from jax import lax
from jax.experimental import pallas as pl
from jax.experimental.pallas import tpu as pltpu
from jax.sharding import PartitionSpec as P

HEADS = 12
BLK = 128
HB = 2
PAIR = 128
HALF = 64
LIMIT = 50 * 2**20
NEG = -1e30
F32 = jnp.float32
BF16 = jnp.bfloat16


def params():
    return pltpu.CompilerParams(vmem_limit_bytes=LIMIT)


def cost(flops, nbytes, trans=0):
    return pl.CostEstimate(flops=int(flops), bytes_accessed=int(nbytes), transcendentals=int(trans))


def struct(rows, cols, dtype=BF16):
    return jax.ShapeDtypeStruct((rows, cols), dtype)


def whole(array):
    return pl.BlockSpec(array.shape, lambda *_: (0,) * array.ndim)


def mm(a, b):
    return jnp.dot(a, b, preferred_element_type=F32)


def mm_t(a, b):
    return lax.dot_general(a, b, (((1,), (1,)), ((), ())), preferred_element_type=F32)


def normed_rows(rows, gain):
    floats = rows.astype(F32)
    factor = lax.rsqrt(jnp.mean(floats * floats, axis=-1, keepdims=True) + 1e-06)
    return (floats * factor * gain).astype(BF16)


def pick_kernel(send_ref, index_ref, points_ref, first_ref, second_ref, prev_ref, next_ref):
    rows = points_ref.shape[0]
    anchors = index_ref.shape[1]
    slot = lax.broadcasted_iota(jnp.int32, (rows, anchors), 0)
    chosen = jnp.where(slot == index_ref[...], 1.0, 0.0).astype(BF16)
    picked = lax.dot_general(
        chosen, points_ref[...], (((0,), (0,)), ((), ())), preferred_element_type=F32
    ).astype(BF16)
    first_ref[...] = picked[: anchors // 2]
    second_ref[...] = picked[anchors // 2 :]
    for place in range(HB):
        for base, out_ref in ((0, prev_ref), (HB, next_ref)):
            start = pl.multiple_of(send_ref[base + place] * BLK, BLK)
            out_ref[place * BLK : (place + 1) * BLK, :] = points_ref[pl.ds(start, BLK), :]


def pick(points, send_blocks, anchor_index):
    rows, width = points.shape
    anchors = anchor_index.shape[0]
    index = anchor_index.reshape(1, anchors)
    half = struct(anchors // 2, width)
    side = struct(HB * BLK, width)
    return pl.pallas_call(
        pick_kernel,
        out_shape=(half, half, side, side),
        grid_spec=pltpu.PrefetchScalarGridSpec(
            num_scalar_prefetch=1,
            grid=(1,),
            in_specs=[whole(index), whole(points)],
            out_specs=[whole(half), whole(half), whole(side), whole(side)],
        ),
        compiler_params=params(),
        cost_estimate=cost(2 * anchors * rows * width, 4 * rows * width),
    )(send_blocks, index, points)


def project_kernel(points_ref, gain_ref, wqkv_ref, wcq_ref, queries_ref, table_ref):
    width = points_ref.shape[1]
    normed = normed_rows(points_ref[...], gain_ref[...])
    scale = HALF**-0.5
    queries = mm(normed, wqkv_ref[:, :width]).astype(BF16)
    queries_ref[:, :width] = (queries.astype(F32) * scale).astype(BF16)
    cross = mm(normed, wcq_ref[...]).astype(BF16)
    queries_ref[:, width:] = (cross.astype(F32) * scale).astype(BF16)
    table_ref[...] = mm(normed, wqkv_ref[:, width:]).astype(BF16)


def project(points, gain, w_qkv, w_cross_q, extra_rows):
    rows, width = points.shape
    tile = 256
    return pl.pallas_call(
        project_kernel,
        out_shape=(struct(rows, 2 * width), struct(rows + extra_rows, 2 * width)),
        grid=(rows // tile,),
        in_specs=[
            pl.BlockSpec((tile, width), lambda i: (i, 0)),
            whole(gain),
            whole(w_qkv),
            whole(w_cross_q),
        ],
        out_specs=[
            pl.BlockSpec((tile, 2 * width), lambda i: (i, 0)),
            pl.BlockSpec((tile, 2 * width), lambda i: (i, 0)),
        ],
        compiler_params=params(),
        cost_estimate=cost(2 * rows * width * 4 * width, 20 * rows * width),
    )(points, gain, w_qkv, w_cross_q)


def remote_kernel(low_ref, high_ref, gain_ref, wqkv_ref, _, table_ref):
    width = low_ref.shape[1]
    side = low_ref.shape[0]
    for place, ref in enumerate((low_ref, high_ref)):
        normed = normed_rows(ref[...], gain_ref[...])
        table_ref[place * side : (place + 1) * side, :] = mm(
            normed, wqkv_ref[:, width:]
        ).astype(BF16)


def project_remote(low, high, gain, w_qkv, table, own_rows):
    side, width = low.shape
    return pl.pallas_call(
        remote_kernel,
        out_shape=struct(*table.shape),
        grid=(1,),
        in_specs=[
            whole(low),
            whole(high),
            whole(gain),
            whole(w_qkv),
            pl.BlockSpec(memory_space=pl.ANY),
        ],
        out_specs=pl.BlockSpec((2 * side, 2 * width), lambda i: (own_rows // (2 * side), 0)),
        input_output_aliases={4: 0},
        compiler_params=params(),
        cost_estimate=cost(8 * side * width * width, 8 * side * width),
    )(low, high, gain, w_qkv, table)


def split_heads(rows):
    lane = lax.broadcasted_iota(jnp.int32, rows.shape, 1)
    zero = jnp.zeros_like(rows)
    return jnp.concatenate(
        [jnp.where(lane < HALF, rows, zero), jnp.where(lane >= HALF, rows, zero)], axis=0
    )


def join_heads(both):
    count = both.shape[0] // 2
    lane = lax.broadcasted_iota(jnp.int32, (count, PAIR), 1)
    return jnp.where(lane < HALF, both[:count], both[count:])


def block_kernel(ids_ref, count_ref, live_ref, queries_ref, table_ref, out_ref):
    block = pl.program_id(0)
    slots = ids_ref.shape[0] // count_ref.shape[0]
    width = queries_ref.shape[1]
    count = count_ref[block]
    pairs = jnp.where(block < live_ref[0], (count + 1) // 2, 0)

    @pl.when(pairs == 0)
    def _():
        out_ref[...] = jnp.zeros_like(out_ref)

    for used in range(1, slots // 2 + 1):

        @pl.when(pairs == used)
        def _(used=used):
            starts = [
                pl.multiple_of(ids_ref[block * slots + n] * BLK, BLK) for n in range(2 * used)
            ]
            ones = jnp.ones((2 * used * BLK, PAIR), BF16)
            last = (2 * used - 1) * BLK
            dropped = jnp.where(count == 2 * used, 0.0, NEG)
            for pair in range(width // PAIR):
                at = pair * PAIR
                keys = jnp.concatenate(
                    [table_ref[pl.ds(s, BLK), at : at + PAIR] for s in starts], axis=0
                )
                values = jnp.concatenate(
                    [table_ref[pl.ds(s, BLK), width + at : width + at + PAIR] for s in starts],
                    axis=0,
                )
                query = split_heads(queries_ref[:, at : at + PAIR])
                scores = mm_t(query, keys)
                scores = jnp.concatenate([scores[:, :last], scores[:, last:] + dropped], axis=1)
                top = jnp.max(scores, axis=1, keepdims=True)
                weights = jnp.exp(scores - top).astype(BF16)
                total = mm(weights, jnp.concatenate([values, ones], axis=1))
                out_ref[:, at : at + PAIR] = join_heads(total[:, :PAIR] / total[:, PAIR:]).astype(
                    BF16
                )


def block_attention(queries, table, ids, counts, live):
    rows = queries.shape[0]
    width = queries.shape[1] // 2
    blocks = rows // BLK
    return pl.pallas_call(
        block_kernel,
        out_shape=struct(rows, width),
        grid_spec=pltpu.PrefetchScalarGridSpec(
            num_scalar_prefetch=3,
            grid=(blocks,),
            in_specs=[
                pl.BlockSpec((BLK, width), lambda i, *_: (i, 0)),
                whole(table),
            ],
            out_specs=pl.BlockSpec((BLK, width), lambda i, *_: (i, 0)),
        ),
        compiler_params=params(),
        cost_estimate=cost(4 * 4 * rows * 5 * BLK * width, 8 * rows * width, rows * 5 * BLK * 12),
    )(ids.reshape(-1), counts, live, queries, table)


def anchor_kernel(rows_ref, gain_ref, weight_ref, out_ref):
    normed = normed_rows(rows_ref[...], gain_ref[...])
    out_ref[...] = mm(normed, weight_ref[...]).astype(BF16)


def anchor_project(rows, gain, weight):
    count, width = rows.shape
    tile = 512
    return pl.pallas_call(
        anchor_kernel,
        out_shape=struct(count, 2 * width),
        grid=(count // tile,),
        in_specs=[pl.BlockSpec((tile, width), lambda i: (i, 0)), whole(gain), whole(weight)],
        out_specs=pl.BlockSpec((tile, 2 * width), lambda i: (i, 0)),
        compiler_params=params(),
        cost_estimate=cost(4 * count * width * width, 6 * count * width),
    )(rows, gain, weight)


CHUNK = 256


def sweep(query, keys_ref, values_ref, top, total):
    ones = jnp.ones((CHUNK, PAIR), BF16)
    for start in range(0, keys_ref.shape[0], CHUNK):
        scores = mm_t(query, keys_ref[start : start + CHUNK, :])
        here = jnp.max(scores, axis=1, keepdims=True)
        values = jnp.concatenate([values_ref[start : start + CHUNK, :], ones], axis=1)
        if top is None:
            top = here
            total = mm(jnp.exp(scores - top).astype(BF16), values)
        else:
            later = jnp.maximum(top, here)
            total = total * jnp.exp(top - later) + mm(
                jnp.exp(scores - later).astype(BF16), values
            )
            top = later
    return top, total


def cross_first_kernel(queries_ref, keys_ref, values_ref, top_ref, sum_ref, acc_ref):
    query = split_heads(queries_ref[...])
    top, total = sweep(query, keys_ref, values_ref, None, None)
    top_ref[...] = join_heads(jnp.broadcast_to(top, (query.shape[0], PAIR)))
    sum_ref[...] = join_heads(total[:, PAIR:])
    acc_ref[...] = join_heads(total[:, :PAIR])


def cross_last_kernel(
    live_ref,
    queries_ref,
    keys_ref,
    values_ref,
    top_ref,
    sum_ref,
    acc_ref,
    block_ref,
    wout_ref,
    wcross_ref,
    out_ref,
    held_ref,
):
    pair = pl.program_id(1)
    rows = queries_ref.shape[0]
    query = split_heads(queries_ref[...])
    tops = top_ref[...]
    top = jnp.concatenate([tops[:, :1], tops[:, HALF : HALF + 1]], axis=0)
    state = jnp.concatenate([acc_ref[...], sum_ref[...]], axis=1)
    total = jnp.concatenate([state, state], axis=0)
    top, total = sweep(query, keys_ref, values_ref, top, total)
    held_ref[pair] = join_heads(total[:, :PAIR] / total[:, PAIR:]).astype(BF16)

    @pl.when(pair == pl.num_programs(1) - 1)
    def _():
        cross = jnp.concatenate([held_ref[n] for n in range(held_ref.shape[0])], axis=1)
        mixed = mm(block_ref[...], wout_ref[...]) + mm(cross, wcross_ref[...])
        place = lax.broadcasted_iota(jnp.int32, (rows, 1), 0) + pl.program_id(0) * rows
        out_ref[...] = jnp.where(place // BLK < live_ref[0], mixed, 0.0).astype(BF16)


def cross_first(queries, anchor_kv):
    rows = queries.shape[0]
    width = queries.shape[1] // 2
    count = anchor_kv.shape[0]
    pairs = width // PAIR
    tile = 512
    state = struct(rows, width, F32)
    spec = pl.BlockSpec((tile, PAIR), lambda h, i: (i, h))
    return pl.pallas_call(
        cross_first_kernel,
        out_shape=(state, state, state),
        grid=(pairs, rows // tile),
        in_specs=[
            pl.BlockSpec((tile, PAIR), lambda h, i: (i, pairs + h)),
            pl.BlockSpec((count, PAIR), lambda h, i: (0, h)),
            pl.BlockSpec((count, PAIR), lambda h, i: (0, pairs + h)),
        ],
        out_specs=[spec, spec, spec],
        compiler_params=params(),
        cost_estimate=cost(16 * rows * count * width, 24 * rows * width, 12 * rows * count),
    )(queries, anchor_kv, anchor_kv)


def cross_last(queries, anchor_kv, state, block_attn, w_out, w_cross_out, live):
    rows = queries.shape[0]
    width = queries.shape[1] // 2
    count = anchor_kv.shape[0]
    pairs = width // PAIR
    tile = 512
    spec = pl.BlockSpec((tile, PAIR), lambda i, h, *_: (i, h))
    full = pl.BlockSpec((tile, width), lambda i, h, *_: (i, 0))
    return pl.pallas_call(
        cross_last_kernel,
        out_shape=struct(rows, width),
        grid_spec=pltpu.PrefetchScalarGridSpec(
            num_scalar_prefetch=1,
            grid=(rows // tile, pairs),
            in_specs=[
                pl.BlockSpec((tile, PAIR), lambda i, h, *_: (i, pairs + h)),
                pl.BlockSpec((count, PAIR), lambda i, h, *_: (0, h)),
                pl.BlockSpec((count, PAIR), lambda i, h, *_: (0, pairs + h)),
                spec,
                spec,
                spec,
                full,
                whole(w_out),
                whole(w_cross_out),
            ],
            out_specs=full,
            scratch_shapes=[pltpu.VMEM((pairs, tile, PAIR), BF16)],
        ),
        compiler_params=params(),
        cost_estimate=cost(16 * rows * count * width, 24 * rows * width, 12 * rows * count),
    )(live, queries, anchor_kv, anchor_kv, *state, block_attn, w_out, w_cross_out)


def local(
    points,
    norm_gain,
    w_qkv,
    w_out,
    w_cross_q,
    w_cross_kv,
    w_cross_out,
    live_blocks,
    send_blocks,
    neighbours,
    neighbour_count,
    anchor_index,
):
    rows, width = points.shape
    gain = norm_gain.reshape(1, width)
    first, second, to_prev, to_next = pick(points, send_blocks, anchor_index)
    size = lax.axis_size("dom")
    forward = [(i, i + 1) for i in range(size - 1)]
    backward = [(i + 1, i) for i in range(size - 1)]
    low = lax.ppermute(to_next, "dom", forward)
    high = lax.ppermute(to_prev, "dom", backward)
    first = lax.all_gather(first, "dom", axis=0, tiled=True)
    second = lax.all_gather(second, "dom", axis=0, tiled=True)
    queries, table = project(points, gain, w_qkv, w_cross_q, 2 * HB * BLK)
    table = project_remote(low, high, gain, w_qkv, table, rows)
    block_attn = block_attention(queries, table, neighbours, neighbour_count, live_blocks)
    state = cross_first(queries, anchor_project(first, gain, w_cross_kv))
    return cross_last(
        queries,
        anchor_project(second, gain, w_cross_kv),
        state,
        block_attn,
        w_out,
        w_cross_out,
        live_blocks,
    )


def solution(mesh):
    sharded = P(("car", "dom"))
    in_specs = (
        P(("car", "dom"), None),
        P(),
        P(),
        P(),
        P(),
        P(),
        P(),
        sharded,
        sharded,
        P(("car", "dom"), None),
        sharded,
        sharded,
    )
    out_specs = P(("car", "dom"), None)
    return jax.shard_map(local, mesh=mesh, in_specs=in_specs, out_specs=out_specs, check_vma=False)
```

time: 413 us -> 192 us (0.46)
  matrix products: 229 us -> 0 us
  Pallas kernels: 0 us -> 157 us
  local copies, waits for them, and re-layouts: 122 us -> 9.74 us
  waiting for transfers between devices: 24.2 us -> 0.72 us
  other arithmetic: 11.4 us -> 0 us
    pallas_call x0 -> x8, Pallas kernels: none -> 157 us  [the longest x1 72.6 us: cross_last(): pl.pallas_call(cross_last_kernel, out_shape=struct(rows, width), grid_spe...]
    dot_general x9 -> x0, matrix products: 119 us -> none  [the longest x4 94.5 us: attend_batch(): jnp.einsum('bhrk,bkhd->brhd', weights, value_heads, preferred_element_typ...]
    sub x4 -> x0, matrix products: 110 us -> none  [attend_batch(): expo = jnp.exp(scores - row_max)]
    while x22 -> x0, local copies, waits for them, and re-layouts: 55.1 us -> none
    slice x6 -> x0, local copies, waits for them, and re-layouts: 36.7 us -> none  [the longest x2 20.7 us: one_group(): tiles[:, :, :model_width]]
    ppermute x2, waiting for transfers between devices: 24.1 us -> 0.01 us  [the longest x1 0.01 us: local(): high = lax.ppermute(to_prev, 'dom', backward)]
    gather x4 -> x0, local copies, waits for them, and re-layouts: 23.9 us -> none  [the longest x2 18.4 us: one_group(): tiles = pair_table[block_ids].reshape(group_size, -1, 2 * model_width)]
    unnamed x16 -> x24, local copies, waits for them, and re-layouts: 1.89 us -> 8.28 us
  transfers between devices with their start and end apart: 3 -> 4, of which waited for: 1 -> 0; matrix products, arithmetic and copies ran while one was open for 39% -> 1% of each run, Pallas kernels for 0% -> 39%
where the time goes in v1:
time: 192 us; the launch traced here: 188 us
  Pallas kernels  157 us (82%)
  between operations  14.1 us (7%)
  local copies, waits for them, and re-layouts  9.74 us (5%)
  starting transfers between devices  6.9 us (4%)
    pallas_call x1, Pallas kernels, cross_last(): pl.pallas_call(cross_last_kernel, out_shape=struct(rows, width), grid_spe...  72.6 us
    pallas_call x1, Pallas kernels, cross_first(): pl.pallas_call(cross_first_kernel, out_shape=(state, state, state), grid=...  35.5 us
    pallas_call x2, Pallas kernels, anchor_project(): pl.pallas_call(anchor_kernel, out_shape=struct(count, 2 * width), grid=(c...  17.3 us
    pallas_call x1, Pallas kernels, block_attention(): pl.pallas_call(block_kernel, out_shape=struct(rows, width), grid_spec=plt...  15.6 us
    pallas_call x1, Pallas kernels, project(): pl.pallas_call(project_kernel, out_shape=(struct(rows, 2 * width), struct...  8.82 us
    unnamed x24, local copies, waits for them, and re-layouts  8.28 us
    ppermute x1, starting transfers between devices, local(): low = lax.ppermute(to_next, 'dom', forward)  4.94 us
    pallas_call x1, Pallas kernels, project_remote(): pl.pallas_call(remote_kernel, out_shape=struct(*table.shape), grid=(1,),...  4.72 us
  transfers between devices with their start and end apart: 4, of which 0 were waited for; matrix products, arithmetic and copies ran while one was open for 1% of the time, Pallas kernels for 39%

profile of v1, /device:TPU:1, one launch (start us, length us, event | category | flops | bytes accessed | tf_op | source)
XLA Modules:
  0.0 188.0 jit_solution(5776741134684477686)
XLA Ops:
  6.5 1.4 copy-done
  7.9 0.7 copy-done.2
  8.6 0.7 copy-done.3
  9.3 1.9 %shard_map.119 = (bf16[128,768]{1,0:T(8,128)(2,1)}, bf16[128,768]{1,0:T(8,128)(2,1)}, bf16[256,768]{1,0:T(8,128)(2,1)S(1)}, bf16[256,768]{1,0:T(8,128)(2,1)S(1)}) custom-call(s32[4]{0:T(128)S(1)} %copy-done.3, s32[1,256]{1,0:T(1,128)S(1)} %bitcast.1, bf16[1024,768]{1,0:T(8,128)(2,1)S(1)} %copy-done), custom_call_target="tpu_custom_call" | custom-call | flops 402653184 | bytes 3145728 | tf_op jit(solution)/shard_map/pallas_call | solution.py:73
  11.2 0.0 all-gather.5.cloned.1.call-update
  11.2 0.0 all-gather.3.cloned.1.call-start
  11.3 0.7 all-gather.3.cloned.1.call-update
  12.0 4.9 %collective-permute-start = (bf16[256,768]{1,0:T(8,128)(2,1)S(1)}, bf16[256,768]{1,0:T(8,128)(2,1)S(1)}, u32[]{:S(2)}, u32[]{:S(2)}) collective-permute-start(bf16[256,768]{1,0:T(8,128)(2,1)S(1)} %get-tuple-element.20), channel_id=1, source_target_pairs={{0,1},{1,2},{2,3},{3,4},{4,5},{5,6},{6,7},{7,8},{8,9},{9,10},{10,1... | collective-permute-start | bytes 1179656 | tf_op jit(solution)/shard_map/ppermute | solution.py:382
  16.9 1.9 %collective-permute-start.1 = (bf16[256,768]{1,0:T(8,128)(2,1)S(1)}, bf16[256,768]{1,0:T(8,128)(2,1)S(1)}, u32[]{:S(2)}, u32[]{:S(2)}) collective-permute-start(bf16[256,768]{1,0:T(8,128)(2,1)S(1)} %get-tuple-element.21), channel_id=1, source_target_pairs={{1,0},{2,1},{3,2},{4,3},{5,4},{6,5},{7,6},{8,7},{9,8},{10,9},{11,1... | collective-permute-start | bytes 1179656 | tf_op jit(solution)/shard_map/ppermute | solution.py:383
  18.9 0.7 reshape.9.gain_ref
  20.2 0.8 reshape.11.ids_ref
  21.0 1.4 copy-done.1
  22.4 1.3 copy-done.5
  23.7 8.8 %shard_map.118 = (bf16[1024,1536]{1,0:T(8,128)(2,1)}, bf16[1536,1536]{1,0:T(8,128)(2,1)}) custom-call(bf16[1024,768]{1,0:T(8,128)(2,1)S(1)} %copy-done.1, f32[1,768]{1,0:T(1,128)S(1)} %reshape.9.gain_ref, bf16[768,2304]{1,0:T(8,128)(2,1)} %wqkv_ref.3, bf16[768,768]{1,0:T(8,128)(2,1)S(1)} %copy-done.5), custom_call_target="tpu_custom_call" | custom-call | flops 4831838208 | bytes 15728640 | tf_op jit(solution)/shard_map/pallas_call | solution.py:101
  32.5 0.0 copy-start.8
  32.5 4.7 %shard_map.123.table_ref = bf16[1536,1536]{1,0:T(8,128)(2,1)} custom-call(bf16[256,768]{1,0:T(8,128)(2,1)S(1)} %collective-permute-done.low_ref, bf16[256,768]{1,0:T(8,128)(2,1)S(1)} %collective-permute-done.1.high_ref, f32[1,768]{1,0:T(1,128)S(1)} %reshape.9.gain_ref, bf16[768,2304]{1,0:T(8,128)(2,1)} %wqkv_ref.3, ...), custom_call_target="tpu_custom_call", output_to_operand_aliasing={{}: (4, {})} | custom-call | flops 1207959552 | bytes 1572864 | tf_op jit(solution)/shard_map/pallas_call | solution.py:132
  37.2 15.6 %shard_map.124.block_ref = bf16[1024,768]{1,0:T(8,128)(2,1)S(1)} custom-call(s32[64]{0:T(128)S(1)} %reshape.11.ids_ref, s32[8]{0:T(128)S(1)} %copy-done.8, s32[1]{0:T(128)S(6)} %copy.15.live_ref, bf16[1024,1536]{1,0:T(8,128)(2,1)} %get-tuple-element.14.queries_ref, bf16[1536,1536]{1,0:T(8,128)(2,1)} %shard_map.123.table_ref), custom_call_target="tpu_custom_call" | custom-call | flops 8053063680 | bytes 6291456 | tf_op jit(solution)/shard_map/pallas_call | solution.py:209
  52.9 0.0 copy-start.9
  52.9 1.1 copy-done.9
  54.0 8.6 %shard_map.121.keys_ref.values_ref = bf16[2048,1536]{1,0:T(8,128)(2,1)} custom-call(bf16[2048,768]{1,0:T(8,128)(2,1)} %all-gather.5.cloned.1.call-done.rows_ref, f32[1,768]{1,0:T(1,128)S(1)} %reshape.9.gain_ref, bf16[768,1536]{1,0:T(8,128)(2,1)S(1)} %copy-done.4), custom_call_target="tpu_custom_call" | custom-call | flops 4831838208 | bytes 9437184 | tf_op jit(solution)/shard_map/pallas_call | solution.py:234
  62.6 35.5 %shard_map.122 = (f32[1024,768]{1,0:T(8,128)S(1)}, f32[1024,768]{1,0:T(8,128)}, f32[1024,768]{1,0:T(8,128)}) custom-call(bf16[1024,1536]{1,0:T(8,128)(2,1)} %get-tuple-element.14.queries_ref, bf16[2048,1536]{1,0:T(8,128)(2,1)} %shard_map.121.keys_ref.values_ref, bf16[2048,1536]{1,0:T(8,128)(2,1)} %shard_map.121.keys_ref.values_ref), custom_call_target="tpu_custom_call" | custom-call | flops 25769803776 | bytes 18874368 | tf_op jit(solution)/shard_map/pallas_call | solution.py:314
  98.1 1.7 copy-done.11
  99.8 8.7 %shard_map.120.keys_ref.values_ref = bf16[2048,1536]{1,0:T(8,128)(2,1)} custom-call(bf16[2048,768]{1,0:T(8,128)(2,1)} %all-gather.3.cloned.1.call-done.rows_ref, f32[1,768]{1,0:T(1,128)S(1)} %reshape.9.gain_ref, bf16[768,1536]{1,0:T(8,128)(2,1)S(1)} %copy-done.4), custom_call_target="tpu_custom_call" | custom-call | flops 4831838208 | bytes 9437184 | tf_op jit(solution)/shard_map/pallas_call | solution.py:234
  108.5 72.6 %shard_map.125 = bf16[1024,768]{1,0:T(8,128)(2,1)} custom-call(s32[1]{0:T(128)S(6)} %copy.15.live_ref, bf16[1024,1536]{1,0:T(8,128)(2,1)} %get-tuple-element.14.queries_ref, bf16[2048,1536]{1,0:T(8,128)(2,1)} %shard_map.120.keys_ref.values_ref, bf16[2048,1536]{1,0:T(8,128)(2,1)} %shard_map.120.keys_ref.values_ref, f32[1024,768]{1,0:T(8,128)} %copy-done.11, ...), custom_call_target="tpu_custom_call" | custom-call | flops 25769803776 | bytes 18874368 | tf_op jit(solution)/shard_map/pallas_call | solution.py:337
  (20 shorter events, 0.0 us)
Async XLA Ops:
  6.5 47.5 %all-gather.5.cloned.1.call-start = ((), (), s32[]{:S(2)}) async-start(), calls=%async_computation.1 | async-start | bytes 3342336 | tf_op jit(solution)/shard_map/all_gather | solution.py:384
  6.5 1.4 copy-start
  7.9 0.7 copy-start.2
  8.6 0.7 copy-start.3
  11.2 88.6 %all-gather.3.cloned.1.call-start = ((), (), s32[]{:S(2)}) async-start(), calls=%async_computation | async-start | bytes 3342336 | tf_op jit(solution)/shard_map/all_gather | solution.py:385
  12.0 20.5 %collective-permute-start = (bf16[256,768]{1,0:T(8,128)(2,1)S(1)}, bf16[256,768]{1,0:T(8,128)(2,1)S(1)}, u32[]{:S(2)}, u32[]{:S(2)}) collective-permute-start(bf16[256,768]{1,0:T(8,128)(2,1)S(1)} %get-tuple-element.20), channel_id=1, source_target_pairs={{0,1},{1,2},{2,3},{3,4},{4,5},{5,6},{6,7},{7,8},{8,9},{9,10},{10,1... | collective-permute-start | bytes 1179656 | tf_op jit(solution)/shard_map/ppermute | solution.py:382
  16.9 15.5 %collective-permute-start.1 = (bf16[256,768]{1,0:T(8,128)(2,1)S(1)}, bf16[256,768]{1,0:T(8,128)(2,1)S(1)}, u32[]{:S(2)}, u32[]{:S(2)}) collective-permute-start(bf16[256,768]{1,0:T(8,128)(2,1)S(1)} %get-tuple-element.21), channel_id=1, source_target_pairs={{1,0},{2,1},{3,2},{4,3},{5,4},{6,5},{7,6},{8,7},{9,8},{10,9},{11,1... | collective-permute-start | bytes 1179656 | tf_op jit(solution)/shard_map/ppermute | solution.py:383
  21.0 1.4 copy-start.1
  22.4 1.3 copy-start.5
  32.5 4.7 %copy-start.8 = (s32[8]{0:T(128)S(1)}, s32[8]{0:T(128)}, u32[]{:S(2)}) copy-start(s32[8]{0:T(128)} %count_ref.1) | copy-start | bytes 100
  37.2 16.8 %copy-start.4 = (bf16[768,1536]{1,0:T(8,128)(2,1)S(1)}, bf16[768,1536]{1,0:T(8,128)(2,1)}, u32[]{:S(2)}) copy-start(bf16[768,1536]{1,0:T(8,128)(2,1)} %weight_ref.3) | copy-start | bytes 7077892
  52.9 1.1 copy-start.9
  98.1 1.7 copy-start.11
  99.8 8.7 %copy-start.6 = (bf16[768,768]{1,0:T(8,128)(2,1)S(1)}, bf16[768,768]{1,0:T(8,128)(2,1)}, u32[]{:S(2)}) copy-start(bf16[768,768]{1,0:T(8,128)(2,1)} %wout_ref.1) | copy-start | bytes 3538948
  99.8 8.7 %copy-start.7 = (bf16[768,768]{1,0:T(8,128)(2,1)S(1)}, bf16[768,768]{1,0:T(8,128)(2,1)}, u32[]{:S(2)}) copy-start(bf16[768,768]{1,0:T(8,128)(2,1)} %wcross_ref.1) | copy-start | bytes 3538948
  99.8 8.7 %copy-start.10 = (bf16[1024,768]{1,0:T(8,128)(2,1)S(1)}, bf16[1024,768]{1,0:T(8,128)(2,1)}, u32[]{:S(2)}) copy-start(bf16[1024,768]{1,0:T(8,128)(2,1)} %copy-done.9) | copy-start | bytes 4718596
Sparse Core Ops, SparseCore 0:
  11.4 39.5 all-gather.4
  52.7 36.0 all-gather.2
